TPU v7x, 768 devices: a whole 4x8x12 slice. The times are simulated.
768 devices in a mesh: rep: 16 (over x_lo, y), fsdp: 48 (over x_hi, z, core).
Axes of the slice: x: 4 (x_hi: 2, x_lo: 2; x = x_hi * 2 + x_lo), y: 8, z: 12, core: 2. Of those that a mesh axis runs over, the one named last changes fastest.
Arguments:
- tokens: bfloat16 [16, 12288, 8192], P('rep', 'fsdp'), may hold values from -6 to 6
- cotangent: bfloat16 [16, 12288, 288], P('rep', 'fsdp'), may hold values from -0.0546875 to 0.0546875
- weights: float32 [16, 2359296], P('rep', 'fsdp'), may hold values from -6 to 6
- start_weights: float32 [2359296], P('fsdp'), may hold values from -6 to 6
- momentum: float32 [2359296], P('fsdp'), may hold values from -6 to 6
Outputs:
- mixed_weights: float32 [16, 2359296], P('rep', 'fsdp')
- new_momentum: float32 [2359296], P('fsdp')
- new_start: float32 [2359296], P('fsdp')
All inputs are finite; a program needn't handle non-finite values.
Results may differ from a plain program's by a relative error of at most 0.007.
Values may be sent and summed in bfloat16 or wider, within the bound.
A program may use at most 64 MiB of HBM per device.

v0:
```python
import jax
import jax.numpy as jnp
from jax import lax
from jax.sharding import PartitionSpec as P

code_limit = 448.0
scale_eps = 1e-06
inner_rate = 0.5
outer_rate = 0.7
nesterov_mu = 0.9
mix_weight = 0.5


def replica_total(code_rows, block_scale):
    decoded = code_rows.astype(jnp.float32) * block_scale.astype(jnp.float32)[:, None]
    return lax.psum(decoded.reshape(-1), "rep")


def body(tokens, cotangent, weights, start_weights, momentum):
    tok_rows = tokens[0]
    cot_rows = cotangent[0]
    shard_len = weights.shape[1]
    delta_rows = (start_weights - weights[0]).reshape(-1, 128)
    block_scale = (jnp.max(jnp.abs(delta_rows), axis=1) / code_limit + scale_eps).astype(
        jnp.bfloat16
    )
    code_rows = (delta_rows / block_scale.astype(jnp.float32)[:, None]).astype(jnp.bfloat16)
    product = lax.dot_general(
        tok_rows, cot_rows, (((0,), (0,)), ((), ())), preferred_element_type=jnp.float32
    )
    flat_part = product.reshape(-1)
    grad = lax.psum_scatter(
        flat_part.reshape(shard_len // 128 * lax.axis_size("fsdp"), 128),
        "fsdp",
        scatter_dimension=0,
        tiled=True,
    ).reshape(-1)
    summed = replica_total(code_rows, block_scale)
    average = summed / lax.axis_size("rep")
    new_momentum = nesterov_mu * momentum + average
    new_start = start_weights - outer_rate * (nesterov_mu * new_momentum + average)
    current = weights[0] - inner_rate * grad
    mixed_weights = mix_weight * current + (1.0 - mix_weight) * new_start
    return (mixed_weights[None], new_momentum, new_start)


def solution(mesh):
    placed = (
        P("rep", "fsdp", None),
        P("rep", "fsdp", None),
        P("rep", "fsdp"),
        P("fsdp"),
        P("fsdp"),
    )
    return jax.shard_map(
        body,
        mesh=mesh,
        in_specs=placed,
        out_specs=(P("rep", "fsdp"), P("fsdp"), P("fsdp")),
        check_vma=False,
    )
```

profile of v0, /device:TPU:16, one launch (start us, length us, event | category | flops | bytes accessed | tf_op | source)
XLA Modules:
  0.0 270.2 jit_solution(12185790706199824179)
XLA Ops:
  8.0 0.0 copy-start
  8.0 0.0 all-reduce.2.cloned.1.call-start
  8.1 1.2 bitcast_reduce_fusion
  9.3 0.8 bitcast_multiply_fusion
  10.1 0.0 all-reduce.2.cloned.1.call-update
  10.1 0.0 reduce-scatter.2.cloned.1.call-start
  10.2 0.0 copy-done
  10.2 9.1 %fusion = f32[8192,288]{1,0:T(8,128)} fusion(bf16[1,256,8192]{2,1,0:T(8,128)(2,1)} %param.5, bf16[1,256,288]{1,2,0:T(8,128)(2,1)S(1)} %copy-done), kind=kOutput, calls=%fused_computation | convolution fusion | flops 1207959552 | bytes 13778944 | tf_op jit(solution)/shard_map/dot_general | solution.py:28
  19.3 14.6 %reshape_reshape.3 = f32[18432,128]{1,0:T(8,128)} reshape(f32[8192,288]{1,0:T(8,128)} %fusion) | data formatting | bytes 18874368 | tf_op jit(solution)/shard_map/reshape;reshape | solution.py:33
  33.9 0.0 copy-start.1
  33.9 0.0 copy-start.2
  33.9 0.0 copy-start.3
  33.9 0.0 reduce-scatter.2.cloned.1.call-update
  33.9 126.6 %all-reduce.2.cloned.1.call-done = f32[49152]{0:T(1024)} async-done(((f32[49152]{0:T(1024)}), f32[49152]{0:T(1024)}) %all-reduce.2.cloned.1.call-update) | async-done | bytes 196624 | tf_op jit(solution)/shard_map/psum | solution.py:16
  160.6 100.3 %reduce-scatter.2.cloned.1.call-done = f32[384,128]{1,0:T(8,128)} async-done(((f32[18432,128]{1,0:T(8,128)}), f32[384,128]{1,0:T(8,128)}) %reduce-scatter.2.cloned.1.call-update) | async-done | bytes 196624 | tf_op jit(solution)/shard_map/reduce_scatter | solution.py:32
  260.8 0.0 copy-done.1
  260.8 0.0 copy-done.2
  260.8 0.0 copy-done.3
  260.8 1.9 fusion.4
  (1 shorter events, 0.0 us)
Async XLA Ops:
  8.0 2.2 copy-start
  8.0 152.5 %all-reduce.2.cloned.1.call-start = ((), (), s32[]{:S(2)}) async-start(), calls=%async_computation.2 | async-start | bytes 393216 | tf_op jit(solution)/shard_map/psum | solution.py:16
  10.1 250.7 %reduce-scatter.2.cloned.1.call-start = ((), (), s32[]{:S(2)}) async-start(), calls=%async_computation.1 | async-start | bytes 9633792 | tf_op jit(solution)/shard_map/reduce_scatter | solution.py:32
  33.9 226.9 %copy-start.1 = (f32[1,49152]{1,0:T(1,128)S(1)}, f32[1,49152]{1,0:T(1,128)}, u32[]{:S(2)}) copy-start(f32[1,49152]{1,0:T(1,128)} %param.7) | copy-start | bytes 589828
  33.9 226.9 %copy-start.2 = (f32[49152]{0:T(1024)S(1)}, f32[49152]{0:T(1024)}, u32[]{:S(2)}) copy-start(f32[49152]{0:T(1024)} %param.8) | copy-start | bytes 589828
  33.9 226.9 %copy-start.3 = (f32[49152]{0:T(1024)S(1)}, f32[49152]{0:T(1024)}, u32[]{:S(2)}) copy-start(f32[49152]{0:T(1024)} %param.9) | copy-start | bytes 589828
Sparse Core Ops, SparseCore 0:
  13.0 147.5 all-reduce.1
Sparse Core Ops, SparseCore 1:
  34.0 226.8 reduce-scatter.1
where the time goes:
time: 271 us; the launch traced here: 270 us
  waiting for transfers between devices  227 us (84%)
  between operations  15.5 us (6%)
  local copies, waits for them, and re-layouts  14.6 us (5%)
  matrix products  9.14 us (3%)
  other arithmetic  3.89 us (1%)
    psum x1, waiting for transfers between devices, replica_total(): return lax.psum(decoded.reshape(-1), 'rep')  127 us
    reduce_scatter x1, waiting for transfers between devices, body(): lax.psum_scatter(flat_part.reshape(shard_len // 128 * lax.axis_size('fsdp...  100 us
    another operation x1, local copies, waits for them, and re-layouts, body(): flat_part.reshape(shard_len // 128 * lax.axis_size('fsdp'), 128)  14.6 us
    dot_general x1, matrix products, body(): lax.dot_general(tok_rows, cot_rows, (((0,), (0,)), ((), ())), preferred_e...  9.14 us
  transfers between devices with their start and end apart: 2, of which 2 were waited for; matrix products, arithmetic and copies ran while one was open for 9% of the time, Pallas kernels for 0%

commit v1 on v0

v1 whole, which is shorter than its diff:
```python
import jax
import jax.numpy as jnp
from jax import lax
from jax.experimental import pallas as pl
from jax.experimental.pallas import tpu as pltpu
from jax.sharding import PartitionSpec as P

code_limit = 448.0
scale_eps = 1e-06
inner_rate = 0.5
outer_rate = 0.7
nesterov_mu = 0.9
mix_weight = 0.5

MESH = pl.DeviceIdType.MESH
NZ = 12
LANES = 128
SHARD = 384
LATE = 192
EARLY = SHARD - LATE
STEPS = (-2, -1, 1, 2)
SPAN = 512
SPANS = 8
HOPS = NZ // 2


def flatten_span(S, flat, lanes):
    A = [[S[j, pl.ds(k, 128, stride=4), :] for j in range(3)] for k in range(4)]
    R = [A[0]] + [[pltpu.roll(A[k][j], 32 * k, 1) for j in range(3)] for k in (1, 2, 3)]
    m32, m64, m96 = lanes < 32, lanes < 64, lanes < 96
    tiles = [
        R[0][0],
        R[0][1],
        jnp.where(m32, R[0][2], R[1][0]),
        jnp.where(m32, R[1][0], R[1][1]),
        jnp.where(m32, R[1][1], jnp.where(m64, R[1][2], R[2][0])),
        jnp.where(m64, R[2][0], R[2][1]),
        jnp.where(m64, R[2][1], jnp.where(m96, R[2][2], R[3][0])),
        jnp.where(m96, R[3][0], R[3][1]),
        jnp.where(m96, R[3][1], R[3][2]),
    ]
    for j in range(9):
        flat[pl.ds(j, 128, stride=9), :] = tiles[j]


def kernel(
    tok_hbm, cot_hbm, w_hbm, s_hbm,
    grad_hbm, avg_hbm,
    tok2, cot2, cot, wv, sv, dec, avg, ry, rx, S, flat, A, B, XB, ring_a, ring_b, Fa, Fb, xa, xb, grad,
    local_sem, tok_send, tok_recv, cot_send, cot_recv, y_send, y_recv, x_send, x_recv,
    near_sem, g_send, g_recv, b_send, b_recv, ra_send, ra_recv, rb_send, rb_recv, fin_send, fin_recv,
):
    f32 = jnp.float32
    NY = ry.shape[0] + 1
    PIECE = SHARD // NY
    rounds = NY // 2 - 1
    rep = lax.axis_index("rep")
    pos = lax.axis_index("fsdp")
    xl, y = rep // NY, rep % NY
    a, z, c = pos // (2 * NZ), (pos % (2 * NZ)) // 2, pos % 2
    own = c == a
    other = jnp.logical_not(own)

    partner = (rep, pos + 1 - 2 * c)
    z_next = (rep, a * 2 * NZ + ((z + 1) % NZ) * 2 + c)
    z_prev = (rep, a * 2 * NZ + ((z + NZ - 1) % NZ) * 2 + c)
    x_near = ((1 - xl) * NY + y, pos)

    def x_far(core):
        return (rep, (1 - a) * 2 * NZ + z * 2 + core)

    def y_peer(d):
        return (xl * NY + (y + d) % NY, pos)

    def remote(src, dst, send, recv, device):
        return pltpu.make_async_remote_copy(
            src_ref=src, dst_ref=dst, send_sem=send, recv_sem=recv, device_id=device, device_id_type=MESH
        )

    w_copy = pltpu.make_async_copy(w_hbm, wv, local_sem.at[0])
    s_copy = pltpu.make_async_copy(s_hbm, sv, local_sem.at[1])
    cot_copy = pltpu.make_async_copy(cot_hbm, cot2.at[:, pl.ds(0, 256)], local_sem.at[2])
    half = SPAN * SPANS
    tok_copy = pltpu.make_async_copy(
        tok_hbm.at[:, pl.ds(pl.multiple_of(c * half, half), half)], tok2.at[pl.ds(0, 256)], local_sem.at[3]
    )
    cot_copy.start()
    tok_copy.start()
    w_copy.start()
    s_copy.start()

    turn = NY // 2
    place = jnp.where(y < turn, y, NY + turn - 1 - y)

    def y_near(o):
        at = place + o
        return (xl * NY + jnp.where(at < turn, at, NY + turn - 1 - at), pos)

    def each_near(act):
        for j, o in enumerate(STEPS):

            @pl.when((place + o >= 0) & (place + o < NY))
            def _():
                act(j, o)

    barrier = pltpu.get_barrier_semaphore()
    for dev in (partner, z_next, z_prev, x_near, x_far(0), x_far(1)):
        pl.semaphore_signal(barrier, inc=1, device_id=dev, device_id_type=MESH)
    each_near(lambda j, o: pl.semaphore_signal(barrier, inc=1, device_id=y_near(o), device_id_type=MESH))
    n_near = jnp.minimum(place, 2) + jnp.minimum(NY - 1 - place, 2)

    def pass_on(r):
        if r < rounds:
            each_near(
                lambda j, o: pl.semaphore_signal(
                    near_sem.at[3 - j, r], inc=1, device_id=y_near(o), device_id_type=MESH
                )
            )

    def heard(r):
        if r < rounds:
            each_near(lambda j, o: pl.semaphore_wait(near_sem.at[j, r], 1))

    far = (z + HOPS) % NZ

    def pick(table, i):
        return sum(jnp.where(i == j, v, 0) for j, v in enumerate(table))

    def span_at(i):
        outer = pick((0, 1, -1, -2, 2, -3, 3, 4), i)
        inner = pick((0, 1, 2, -1, 3, -2, 4, -3), i)
        third = far % 3
        o = jnp.where(third == 1, inner, jnp.where(third == 0, outer, 1 - outer))
        return (2 * (far // 3) + o + 2 * SPANS) % SPANS

    def tok_remote(i):
        t = span_at(i)
        return remote(
            tok_hbm.at[:, pl.ds(pl.multiple_of((1 - c) * half + t * SPAN, SPAN), SPAN)],
            tok2.at[pl.ds(256, 256), pl.ds(pl.multiple_of(t * SPAN, SPAN), SPAN)],
            tok_send.at[i],
            tok_recv.at[i],
            partner,
        )

    cot_remote = remote(cot_hbm, cot2.at[:, pl.ds(256, 256)], cot_send, cot_recv, partner)

    def y_remote(d):
        return remote(
            dec.at[pl.ds(pl.multiple_of(((y + d) % NY) * PIECE, 8), PIECE)],
            ry.at[d - 1],
            y_send.at[d - 1],
            y_recv.at[d - 1],
            y_peer(d),
        )

    mine = pl.ds(pl.multiple_of(y * PIECE, 8), PIECE)
    x_remote = remote(rx.at[0], rx.at[1], x_send, x_recv, x_near)

    def g_remote(d):
        return remote(avg.at[mine], avg.at[mine], g_send.at[d - 1], g_recv.at[d - 1], y_peer(d))

    def b_remote(i):
        rows = pl.ds(3 * span_at(i), 3)
        return remote(B.at[rows], XB.at[rows], b_send.at[i], b_recv.at[i], x_far(c))

    def dest_at(way, s):
        return (z + HOPS - s) % NZ if way == 0 else (z + NZ - HOPS + s) % NZ

    def ring_remote(P_, way, k, s):
        buf, ring, send, recv = P_
        return remote(
            buf.at[dest_at(way, s) * 2 + k],
            ring.at[way, k, s],
            send.at[way, k, s],
            recv.at[way, k, s],
            z_next if way == 0 else z_prev,
        )

    part_a = (A, ring_a, ra_send, ra_recv)
    part_b = (B, ring_b, rb_send, rb_recv)
    order = ((0, 0), (1, 1), (1, 0), (0, 1))

    def ring_step(P_, way, k, s):
        buf, ring = P_[:2]
        ring_remote(P_, way, k, s - 1).wait_recv()
        at = dest_at(way, s) * 2 + k
        buf[at] = (buf[at].astype(f32) + ring[way, k, s - 1].astype(f32)).astype(buf.dtype)
        ring_remote(P_, way, k, s).start()
        ring_remote(P_, way, k, s - 1).wait_send()

    def ring_0(P_):
        ring_remote(P_, 0, 0, 0).start()
        ring_remote(P_, 1, 1, 0).start()

    def ring_1(P_):
        ring_remote(P_, 0, 1, 1).start()
        ring_remote(P_, 1, 0, 1).start()
        ring_step(P_, 0, 0, 1)
        ring_step(P_, 1, 1, 1)

    def ring_s(P_, s):
        for way, k in order:
            ring_step(P_, way, k, s)

    lanes = lax.broadcasted_iota(jnp.int32, (128, LANES), 1)

    def do_spans(lo, hi):
        @pl.loop(lo, hi)
        def _(i):
            t = span_at(i)
            tok_remote(i).wait_recv()
            for q in range(4):
                X = tok2[:, pl.ds(pl.multiple_of(t * SPAN + 128 * q, 128), 128)]
                out = lax.dot_general(X, cot[...], (((0,), (0,)), ((), ())), preferred_element_type=f32)
                for j in range(2):
                    S[j, 128 * q : 128 * q + 128, :] = out[:, 128 * j : 128 * j + 128]
                S[2, 128 * q : 128 * q + 128, 0:32] = out[:, 256:288]
            flatten_span(S, flat, lanes)
            for j in range(3):
                A[3 * t + j] = flat[SHARD * j : SHARD * j + LATE, :].astype(A.dtype)
                B[3 * t + j] = flat[SHARD * j + LATE : SHARD * (j + 1), :].astype(B.dtype)

            @pl.when(other)
            def _():
                b_remote(i).start()

    def add_spans(lo, hi):
        @pl.loop(lo, hi)
        def _(i):
            t = span_at(i)
            b_remote(i).wait_recv()
            for j in range(3):
                B[3 * t + j] = (B[3 * t + j].astype(f32) + XB[3 * t + j].astype(f32)).astype(B.dtype)

    pl.semaphore_wait(barrier, 6 + n_near)
    cot_remote.start()

    @pl.loop(0, SPANS)
    def _(i):
        tok_remote(i).start()

    pass_on(0)
    S[2] = jnp.zeros((SPAN, LANES), f32)
    tok_copy.wait()
    cot_copy.wait()
    cot_remote.wait_recv()
    cot[...] = cot2[...].astype(f32).T.astype(cot.dtype)

    do_spans(0, 2)
    ring_0(part_a)
    heard(0)
    pass_on(1)

    w_copy.wait()
    s_copy.wait()
    delta = sv[...] - wv[...]
    scale = (jnp.max(jnp.abs(delta), axis=1, keepdims=True) / code_limit + scale_eps).astype(jnp.bfloat16)
    scale = scale.astype(f32)
    dec[...] = (delta / scale).astype(jnp.bfloat16).astype(f32) * scale

    do_spans(2, 3)
    ring_1(part_a)
    do_spans(3, 6)
    heard(1)
    pass_on(2)

    @pl.when(own)
    def _():
        add_spans(0, 2)
        ring_0(part_b)

    ring_s(part_a, 2)
    do_spans(6, 8)

    @pl.when(own)
    def _():
        add_spans(2, 3)
        ring_1(part_b)

    ring_s(part_a, 3)
    heard(2)

    @pl.loop(1, NY)
    def _(d):
        y_remote(d).start()

    @pl.when(own)
    def _():
        add_spans(3, 4)
        ring_s(part_b, 2)

    ring_s(part_a, 4)

    @pl.loop(0, SPANS)
    def _(i):
        tok_remote(i).wait_send()

    cot_remote.wait_send()

    @pl.when(own)
    def _():
        add_spans(4, 6)
        ring_s(part_b, 3)

    ring_s(part_a, 5)

    @pl.loop(1, NY)
    def _(d):
        y_remote(d).wait()

    total = dec[mine, :]
    for d in range(NY - 1):
        total = total + ry[d]
    rx[0] = total
    x_remote.start()

    @pl.when(own)
    def _():
        add_spans(6, 7)
        ring_s(part_b, 4)

    def spread():
        x_remote.wait()
        avg[mine, :] = (rx[0] + rx[1]) / (2 * NY)

        @pl.loop(1, NY)
        def _(d):
            g_remote(d).start()

    @pl.when(own)
    def _():
        spread()
        add_spans(7, 8)
        ring_s(part_b, 5)

    def fin(P_, k, slot, dst, device):
        return remote((Fa if P_ is part_a else Fb).at[k], dst, fin_send.at[slot], fin_recv.at[slot], device)

    def a_partner(k):
        return fin(part_a, k, 0, xa.at[0], partner)

    def a_far(k):
        return remote(Fa.at[k], xa.at[1], fin_send.at[1 + k], fin_recv.at[1], x_far(k))

    def b_partner(k):
        return fin(part_b, k, 3, xb, partner)

    def finish(P_, k):
        buf, ring = P_[:2]
        ring_remote(P_, 0, k, HOPS - 1).wait_recv()
        ring_remote(P_, 1, k, HOPS - 1).wait_recv()
        return buf[z * 2 + k].astype(f32) + ring[0, k, HOPS - 1].astype(f32) + ring[1, k, HOPS - 1].astype(f32)

    near_first = jnp.where(own, 1 - c, 0)
    for k in (near_first, 1 - near_first):
        Fa[k] = finish(part_a, k).astype(Fa.dtype)

        @pl.when(other)
        def _():
            a_far(k).start()

        @pl.when(own & (c != k))
        def _():
            a_partner(k).start()

    @pl.when(other)
    def _():
        spread()

    @pl.when(own)
    def _():
        Fb[1 - c] = finish(part_b, 1 - c).astype(Fb.dtype)
        b_partner(1 - c).start()
        grad[LATE:, :] = finish(part_b, c)

    a_far(0).wait_recv()

    @pl.when(own)
    def _():
        grad[:LATE, :] = Fa[c].astype(f32) + xa[1].astype(f32)

    @pl.when(other)
    def _():
        a_partner(0).wait_recv()
        grad[:LATE, :] = xa[0].astype(f32) + xa[1].astype(f32)
        b_partner(0).wait_recv()
        grad[LATE:, :] = xb[...].astype(f32)

    grad_copy = pltpu.make_async_copy(grad, grad_hbm, local_sem.at[5])
    grad_copy.start()

    @pl.loop(1, NY)
    def _(d):
        g_remote(d).wait()

    avg_copy = pltpu.make_async_copy(avg, avg_hbm, local_sem.at[4])
    avg_copy.start()

    def ring_sent(P_):
        for way, k in order:
            ring_remote(P_, way, k, HOPS - 1).wait_send()

    ring_sent(part_a)

    @pl.when(own)
    def _():
        a_partner(0).wait_send()
        b_partner(0).wait_send()
        ring_sent(part_b)

    @pl.when(other)
    def _():
        a_far(0).wait_send()
        a_far(1).wait_send()

        @pl.loop(0, SPANS)
        def _(i):
            b_remote(i).wait_send()

    avg_copy.wait()
    grad_copy.wait()


def body(tokens, cotangent, weights, start_weights, momentum):
    shape = (SHARD, LANES)
    ny = lax.axis_size("rep") // 2
    piece = SHARD // ny
    f32, bf16 = jnp.float32, jnp.bfloat16
    dma = pltpu.SemaphoreType.DMA
    out = jax.ShapeDtypeStruct(shape, f32)
    late, early = (LATE, LANES), (EARLY, LANES)
    shards = 2 * NZ
    grad, average = pl.pallas_call(
        kernel,
        out_shape=(out, out),
        in_specs=[pl.BlockSpec(memory_space=pltpu.HBM)] * 4,
        out_specs=[pl.BlockSpec(memory_space=pltpu.HBM)] * 2,
        scratch_shapes=[
            pltpu.VMEM((512, SPAN * SPANS), bf16),
            pltpu.VMEM((288, 512), bf16),
            pltpu.VMEM((512, 288), bf16),
            pltpu.VMEM(shape, f32),
            pltpu.VMEM(shape, f32),
            pltpu.VMEM(shape, f32),
            pltpu.VMEM(shape, f32),
            pltpu.VMEM((ny - 1, piece, LANES), f32),
            pltpu.VMEM((2, piece, LANES), f32),
            pltpu.VMEM((3, SPAN, LANES), f32),
            pltpu.VMEM((1152, LANES), f32),
            pltpu.VMEM((shards, *late), bf16),
            pltpu.VMEM((shards, *early), bf16),
            pltpu.VMEM((shards, *early), bf16),
            pltpu.VMEM((2, 2, HOPS, *late), bf16),
            pltpu.VMEM((2, 2, HOPS, *early), bf16),
            pltpu.VMEM((2, *late), bf16),
            pltpu.VMEM((2, *early), bf16),
            pltpu.VMEM((2, *late), bf16),
            pltpu.VMEM(early, bf16),
            pltpu.VMEM(shape, f32),
            dma((6,)),
            dma((SPANS,)),
            dma((SPANS,)),
            dma,
            dma,
            dma((ny - 1,)),
            dma((ny - 1,)),
            dma,
            dma,
            pltpu.SemaphoreType.REGULAR((len(STEPS), max(ny // 2 - 1, 1))),
            dma((ny - 1,)),
            dma((ny - 1,)),
            dma((SPANS,)),
            dma((SPANS,)),
            dma((2, 2, HOPS)),
            dma((2, 2, HOPS)),
            dma((2, 2, HOPS)),
            dma((2, 2, HOPS)),
            dma((4,)),
            dma((4,)),
        ],
        compiler_params=pltpu.CompilerParams(
            collective_id=0, has_side_effects=True, vmem_limit_bytes=60 << 20
        ),
    )(tokens[0], cotangent[0].T, weights.reshape(shape), start_weights.reshape(shape))
    grad, average = grad.reshape(-1), average.reshape(-1)
    new_momentum = nesterov_mu * momentum + average
    new_start = start_weights - outer_rate * (nesterov_mu * new_momentum + average)
    current = weights[0] - inner_rate * grad
    mixed_weights = mix_weight * current + (1.0 - mix_weight) * new_start
    return mixed_weights[None], new_momentum, new_start


def solution(mesh):
    placed = (
        P("rep", "fsdp", None),
        P("rep", "fsdp", None),
        P("rep", "fsdp"),
        P("fsdp"),
        P("fsdp"),
    )
    return jax.shard_map(
        body,
        mesh=mesh,
        in_specs=placed,
        out_specs=(P("rep", "fsdp"), P("fsdp"), P("fsdp")),
        check_vma=False,
    )
```

time: 271 us -> 54.2 us (0.20)
  the two profiles are of different devices: /device:TPU:16 before, /device:TPU:1 now
where the time goes in v1:
time: 54.2 us; the launch traced here: 54.1 us
  Pallas kernels  51.5 us (95%)
  other arithmetic  1.88 us (3%)
  between operations  0.69 us (1%)
    pallas_call x1, Pallas kernels, body(): pl.pallas_call(kernel, out_shape=(out, out), in_specs=[pl.BlockSpec(memor...  51.5 us
    add x1, other arithmetic, body(): mixed_weights = mix_weight * current + (1.0 - mix_weight) * new_start  1.88 us

profile of v1, /device:TPU:1, one launch (start us, length us, event | category | flops | bytes accessed | tf_op | source)
XLA Modules:
  0.0 54.1 jit_solution(1521084159265430720)
XLA Ops:
  0.6 0.0 copy-start.1
  0.6 0.0 copy-start
  0.7 0.0 copy-start.2
  0.7 51.5 %shard_map.76 = (f32[384,128]{1,0:T(8,128)}, f32[384,128]{1,0:T(8,128)}) custom-call(bf16[256,8192]{1,0:T(8,128)(2,1)} %bitcast.23, bf16[288,256]{1,0:T(8,128)(2,1)} %bitcast.28, f32[384,128]{1,0:T(8,128)} %bitcast.24, f32[384,128]{1,0:T(8,128)} %bitcast.26), custom_call_target="tpu_custom_call" | custom-call | tf_op jit(solution)/shard_map/pallas_call | solution.py:434
  52.2 0.0 copy-done.1
  52.2 0.0 copy-done
  52.2 0.0 copy-done.2
  52.2 1.9 %fusion.3 = (f32[49152]{0:T(1024)}, f32[49152]{0:T(1024)}, f32[49152]{0:T(1024)}) fusion(f32[49152]{0:T(1024)S(1)} %bitcast.25, f32[384,128]{1,0:T(8,128)} %get-tuple-element.5, f32[49152]{0:T(1024)S(1)} %copy-done.1, f32[384,128]{1,0:T(8,128)} %get-tuple-element.6, f32[49152]{0:T(1024)S(1)} %copy-done.2), kind=kLoop, calls=%fused_computation.6 | loop fusion | flops 491520 | bytes 1572864 | tf_op jit(solution)/shard_map/add | solution.py:490
Async XLA Ops:
  0.6 51.5 %copy-start.1 = (f32[49152]{0:T(1024)S(1)}, f32[49152]{0:T(1024)}, u32[]{:S(2)}) copy-start(f32[49152]{0:T(1024)} %param.8) | copy-start | bytes 589828
  0.6 51.5 %copy-start = (f32[1,49152]{1,0:T(1,128)S(1)}, f32[1,49152]{1,0:T(1,128)}, u32[]{:S(2)}) copy-start(f32[1,49152]{1,0:T(1,128)} %param.7) | copy-start | bytes 589828
  0.7 51.5 %copy-start.2 = (f32[49152]{0:T(1024)S(1)}, f32[49152]{0:T(1024)}, u32[]{:S(2)}) copy-start(f32[49152]{0:T(1024)} %param.9) | copy-start | bytes 589828

commit v2 on v1

--- a/solution.py
+++ b/solution.py
@@ -249,8 +249,6 @@
 
     do_spans(0, 2)
     ring_0(part_a)
-    heard(0)
-    pass_on(1)
 
     w_copy.wait()
     s_copy.wait()
@@ -261,16 +259,18 @@
 
     do_spans(2, 3)
     ring_1(part_a)
+    heard(0)
+    pass_on(1)
     do_spans(3, 6)
+
+    @pl.when(own)
+    def _():
+        add_spans(0, 2)
+        ring_0(part_b)
+
+    ring_s(part_a, 2)
     heard(1)
     pass_on(2)
-
-    @pl.when(own)
-    def _():
-        add_spans(0, 2)
-        ring_0(part_b)
-
-    ring_s(part_a, 2)
     do_spans(6, 8)
 
     @pl.when(own)

time: 54.2 us -> 54.3 us (level)
  no operation moved by 1% of the time
where the time goes in v2:
time: 54.3 us; the launch traced here: 54.1 us
  Pallas kernels  51.6 us (95%)
  other arithmetic  1.88 us (3%)
  between operations  0.69 us (1%)
    pallas_call x1, Pallas kernels, body(): pl.pallas_call(kernel, out_shape=(out, out), in_specs=[pl.BlockSpec(memor...  51.6 us
    add x1, other arithmetic, body(): mixed_weights = mix_weight * current + (1.0 - mix_weight) * new_start  1.88 us

profile of v2, /device:TPU:1, one launch (start us, length us, event | category | flops | bytes accessed | tf_op | source)
XLA Modules:
  0.0 54.1 jit_solution(13776274937246804395)
XLA Ops:
  0.6 0.0 copy-start.1
  0.6 0.0 copy-start
  0.7 0.0 copy-start.2
  0.7 51.6 %shard_map.76 = (f32[384,128]{1,0:T(8,128)}, f32[384,128]{1,0:T(8,128)}) custom-call(bf16[256,8192]{1,0:T(8,128)(2,1)} %bitcast.23, bf16[288,256]{1,0:T(8,128)(2,1)} %bitcast.28, f32[384,128]{1,0:T(8,128)} %bitcast.24, f32[384,128]{1,0:T(8,128)} %bitcast.26), custom_call_target="tpu_custom_call" | custom-call | tf_op jit(solution)/shard_map/pallas_call | solution.py:434
  52.2 0.0 copy-done.1
  52.2 0.0 copy-done
  52.3 0.0 copy-done.2
  52.3 1.9 %fusion.3 = (f32[49152]{0:T(1024)}, f32[49152]{0:T(1024)}, f32[49152]{0:T(1024)}) fusion(f32[49152]{0:T(1024)S(1)} %bitcast.25, f32[384,128]{1,0:T(8,128)} %get-tuple-element.5, f32[49152]{0:T(1024)S(1)} %copy-done.1, f32[384,128]{1,0:T(8,128)} %get-tuple-element.6, f32[49152]{0:T(1024)S(1)} %copy-done.2), kind=kLoop, calls=%fused_computation.6 | loop fusion | flops 491520 | bytes 1572864 | tf_op jit(solution)/shard_map/add | solution.py:490
Async XLA Ops:
  0.6 51.6 %copy-start.1 = (f32[49152]{0:T(1024)S(1)}, f32[49152]{0:T(1024)}, u32[]{:S(2)}) copy-start(f32[49152]{0:T(1024)} %param.8) | copy-start | bytes 589828
  0.6 51.6 %copy-start = (f32[1,49152]{1,0:T(1,128)S(1)}, f32[1,49152]{1,0:T(1,128)}, u32[]{:S(2)}) copy-start(f32[1,49152]{1,0:T(1,128)} %param.7) | copy-start | bytes 589828
  0.7 51.6 %copy-start.2 = (f32[49152]{0:T(1024)S(1)}, f32[49152]{0:T(1024)}, u32[]{:S(2)}) copy-start(f32[49152]{0:T(1024)} %param.9) | copy-start | bytes 589828

commit v3 on v2

--- a/solution.py
+++ b/solution.py
@@ -77,6 +77,26 @@
             src_ref=src, dst_ref=dst, send_sem=send, recv_sem=recv, device_id=device, device_id_type=MESH
         )
 
+    turn = NY // 2
+    place = jnp.where(y < turn, y, NY + turn - 1 - y)
+
+    def y_near(o):
+        at = place + o
+        return (xl * NY + jnp.where(at < turn, at, NY + turn - 1 - at), pos)
+
+    def each_near(act):
+        for j, o in enumerate(STEPS):
+
+            @pl.when((place + o >= 0) & (place + o < NY))
+            def _():
+                act(j, o)
+
+    barrier = pltpu.get_barrier_semaphore()
+    for dev in (partner, z_next, z_prev, x_near, x_far(0), x_far(1)):
+        pl.semaphore_signal(barrier, inc=1, device_id=dev, device_id_type=MESH)
+    each_near(lambda j, o: pl.semaphore_signal(barrier, inc=1, device_id=y_near(o), device_id_type=MESH))
+    n_near = jnp.minimum(place, 2) + jnp.minimum(NY - 1 - place, 2)
+
     w_copy = pltpu.make_async_copy(w_hbm, wv, local_sem.at[0])
     s_copy = pltpu.make_async_copy(s_hbm, sv, local_sem.at[1])
     cot_copy = pltpu.make_async_copy(cot_hbm, cot2.at[:, pl.ds(0, 256)], local_sem.at[2])
@@ -88,26 +108,6 @@
     tok_copy.start()
     w_copy.start()
     s_copy.start()
-
-    turn = NY // 2
-    place = jnp.where(y < turn, y, NY + turn - 1 - y)
-
-    def y_near(o):
-        at = place + o
-        return (xl * NY + jnp.where(at < turn, at, NY + turn - 1 - at), pos)
-
-    def each_near(act):
-        for j, o in enumerate(STEPS):
-
-            @pl.when((place + o >= 0) & (place + o < NY))
-            def _():
-                act(j, o)
-
-    barrier = pltpu.get_barrier_semaphore()
-    for dev in (partner, z_next, z_prev, x_near, x_far(0), x_far(1)):
-        pl.semaphore_signal(barrier, inc=1, device_id=dev, device_id_type=MESH)
-    each_near(lambda j, o: pl.semaphore_signal(barrier, inc=1, device_id=y_near(o), device_id_type=MESH))
-    n_near = jnp.minimum(place, 2) + jnp.minimum(NY - 1 - place, 2)
 
     def pass_on(r):
         if r < rounds:
@@ -241,14 +241,6 @@
         tok_remote(i).start()
 
     pass_on(0)
-    S[2] = jnp.zeros((SPAN, LANES), f32)
-    tok_copy.wait()
-    cot_copy.wait()
-    cot_remote.wait_recv()
-    cot[...] = cot2[...].astype(f32).T.astype(cot.dtype)
-
-    do_spans(0, 2)
-    ring_0(part_a)
 
     w_copy.wait()
     s_copy.wait()
@@ -256,6 +248,15 @@
     scale = (jnp.max(jnp.abs(delta), axis=1, keepdims=True) / code_limit + scale_eps).astype(jnp.bfloat16)
     scale = scale.astype(f32)
     dec[...] = (delta / scale).astype(jnp.bfloat16).astype(f32) * scale
+
+    S[2] = jnp.zeros((SPAN, LANES), f32)
+    tok_copy.wait()
+    cot_copy.wait()
+    cot_remote.wait_recv()
+    cot[...] = cot2[...].astype(f32).T.astype(cot.dtype)
+
+    do_spans(0, 2)
+    ring_0(part_a)
 
     do_spans(2, 3)
     ring_1(part_a)

time: 54.3 us -> 54.5 us (level)
  no operation moved by 1% of the time
where the time goes in v3:
time: 54.5 us; the launch traced here: 54.4 us
  Pallas kernels  51.8 us (95%)
  other arithmetic  1.88 us (3%)
  between operations  0.69 us (1%)
    pallas_call x1, Pallas kernels, body(): pl.pallas_call(kernel, out_shape=(out, out), in_specs=[pl.BlockSpec(memor...  51.8 us
    add x1, other arithmetic, body(): mixed_weights = mix_weight * current + (1.0 - mix_weight) * new_start  1.88 us

profile of v3, /device:TPU:1, one launch (start us, length us, event | category | flops | bytes accessed | tf_op | source)
XLA Modules:
  0.0 54.4 jit_solution(6139991100758524213)
XLA Ops:
  0.6 0.0 copy-start.1
  0.6 0.0 copy-start
  0.7 0.0 copy-start.2
  0.7 51.8 %shard_map.76 = (f32[384,128]{1,0:T(8,128)}, f32[384,128]{1,0:T(8,128)}) custom-call(bf16[256,8192]{1,0:T(8,128)(2,1)} %bitcast.23, bf16[288,256]{1,0:T(8,128)(2,1)} %bitcast.28, f32[384,128]{1,0:T(8,128)} %bitcast.24, f32[384,128]{1,0:T(8,128)} %bitcast.26), custom_call_target="tpu_custom_call" | custom-call | tf_op jit(solution)/shard_map/pallas_call | solution.py:435
  52.4 0.0 copy-done.1
  52.5 0.0 copy-done
  52.5 0.0 copy-done.2
  52.5 1.9 %fusion.3 = (f32[49152]{0:T(1024)}, f32[49152]{0:T(1024)}, f32[49152]{0:T(1024)}) fusion(f32[49152]{0:T(1024)S(1)} %bitcast.25, f32[384,128]{1,0:T(8,128)} %get-tuple-element.5, f32[49152]{0:T(1024)S(1)} %copy-done.1, f32[384,128]{1,0:T(8,128)} %get-tuple-element.6, f32[49152]{0:T(1024)S(1)} %copy-done.2), kind=kLoop, calls=%fused_computation.6 | loop fusion | flops 491520 | bytes 1572864 | tf_op jit(solution)/shard_map/add | solution.py:491
Async XLA Ops:
  0.6 51.8 %copy-start.1 = (f32[49152]{0:T(1024)S(1)}, f32[49152]{0:T(1024)}, u32[]{:S(2)}) copy-start(f32[49152]{0:T(1024)} %param.8) | copy-start | bytes 589828
  0.6 51.8 %copy-start = (f32[1,49152]{1,0:T(1,128)S(1)}, f32[1,49152]{1,0:T(1,128)}, u32[]{:S(2)}) copy-start(f32[1,49152]{1,0:T(1,128)} %param.7) | copy-start | bytes 589828
  0.7 51.8 %copy-start.2 = (f32[49152]{0:T(1024)S(1)}, f32[49152]{0:T(1024)}, u32[]{:S(2)}) copy-start(f32[49152]{0:T(1024)} %param.9) | copy-start | bytes 589828
